TPU v7x, 32 devices: a whole 2x2x4 slice. The times are simulated.
32 devices in a mesh: dfa: 8 (over y, x, core), hid: 4 (over z).
Axes of the slice: x: 2, y: 2, z: 4, core: 2. Of those that a mesh axis runs over, the one named last changes fastest.
Arguments:
- beta_last: bfloat16 [256, 8, 4, 1024], P('dfa', None, 'hid'), may hold values from -6 to 6
- transition: bfloat16 [8, 4, 1024, 32768], P(None, 'hid', None, 'dfa'), may hold values from -0.03125 to 0.03125
- emission: bfloat16 [64, 4, 8192], P(None, 'hid'), may hold values from 0.049804688 to 0.59765625
- successor: int32 [256, 8], replicated, may hold values from 0 to 255
- token_set: int32 [256, 8], replicated, may hold values from 0 to 63
Outputs:
- table: bfloat16 [2, 256, 8, 4, 1024], P(None, 'dfa', None, 'hid')
All inputs are finite; a program needn't handle non-finite values.
Results may differ from a plain program's by a relative error of at most 0.0056.
Values may be sent and summed in bfloat16 or wider, within the bound.
A program may use at most 128 MiB of HBM per device.

v0:
```python
import jax
import jax.numpy as jnp
from jax import lax
from jax.sharding import PartitionSpec as P

POS = 2


def edge_mix(beta, emission_own, successor, token_set):
    states, nsets = beta.shape[0], emission_own.shape[0]
    total = jnp.zeros(beta.shape, jnp.float32)
    for column in range(successor.shape[1]):
        pick = (successor[:, column][:, None] == jnp.arange(states)[None, :]).astype(jnp.bfloat16)
        kind = (token_set[:, column][:, None] == jnp.arange(nsets)[None, :]).astype(jnp.bfloat16)
        picked = jnp.dot(pick, beta, preferred_element_type=jnp.float32)
        weights = jnp.dot(kind, emission_own, preferred_element_type=jnp.float32)
        total = total + weights * picked
    return total.astype(jnp.bfloat16)


def local(beta_last, transition, emission, successor, token_set):
    owned, blocks, _, cells = beta_last.shape
    width = blocks * cells
    trans_block = transition.reshape(width, transition.shape[3])
    first = lax.axis_index("dfa") * cells
    emission_own = lax.dynamic_slice_in_dim(emission[:, 0, :], first, cells, 1)
    beta = lax.all_to_all(
        beta_last.reshape(owned, width), "dfa", split_axis=1, concat_axis=0, tiled=True
    )
    results = []
    for position in range(POS):
        mixed_own = edge_mix(beta, emission_own, successor, token_set)
        mixed = lax.all_gather(mixed_own, "dfa", axis=1, tiled=True)
        part = jnp.dot(mixed, trans_block, preferred_element_type=jnp.float32)
        beta = lax.psum_scatter(part, "hid", scatter_dimension=1, tiled=True).astype(jnp.bfloat16)
        own_rows = lax.all_to_all(beta, "dfa", split_axis=0, concat_axis=1, tiled=True)
        results = [own_rows.reshape(owned, blocks, 1, cells)] + results
    return jnp.stack(results)


def solution(mesh):
    return jax.shard_map(
        local,
        mesh=mesh,
        in_specs=(
            P("dfa", None, "hid", None),
            P(None, "hid", None, "dfa"),
            P(None, "hid", None),
            P(),
            P(),
        ),
        out_specs=P(None, "dfa", None, "hid", None),
        check_vma=False,
    )
```

profile of v0, /device:TPU:0, one launch (start us, length us, event | category | flops | bytes accessed | tf_op | source)
XLA Modules:
  0.0 355.7 jit_solution(14288932602628723117)
XLA Ops:
  6.5 2.2 copy.14
  8.8 5.2 %all-to-all-start = ((bf16[32,8,1024]{2,0,1:T(8,128)(2,1)}), bf16[32,8,1024]{2,0,1:T(8,128)(2,1)S(1)}, u32[]{:S(2)}, u32[]{:S(2)}) async-start(bf16[32,8,1024]{2,0,1:T(8,128)(2,1)} %bitcast.67), calls=%async_computation | async-start | bytes 1048576 | tf_op jit(solution)/shard_map/all_to_all | solution.py:27
  16.3 1.4 fusion.16
  19.1 1.4 fusion.24
  23.4 1.3 fusion.18
  25.2 1.7 fusion.13
  31.0 38.5 %all-gather.3.cloned.1.call-done = bf16[256,8192]{1,0:T(8,128)(2,1)} async-done(((bf16[256,1024]{1,0:T(8,128)(2,1)}), bf16[256,8192]{1,0:T(8,128)(2,1)}) %all-gather.3.cloned.1.call-update) | async-done | bytes 4194320 | tf_op jit(solution)/shard_map/all_gather | solution.py:33
  69.5 28.5 %fusion.74 = f32[256,4096]{1,0:T(8,128)} fusion(bf16[256,8192]{1,0:T(8,128)(2,1)} %all-gather.3.cloned.1.call-done, bf16[8192,4096]{1,0:T(8,128)(2,1)} %bitcast.21), kind=kOutput, calls=%fused_computation.108 | convolution fusion | flops 17179869184 | bytes 75497472 | tf_op jit(solution)/shard_map/dot_general | solution.py:34
  98.0 76.9 %reduce-scatter.3.cloned.1.call-done = f32[256,1024]{1,0:T(8,128)} async-done(((f32[256,4096]{1,0:T(8,128)}), f32[256,1024]{1,0:T(8,128)}) %reduce-scatter.3.cloned.1.call-update) | async-done | bytes 1048592 | tf_op jit(solution)/shard_map/reduce_scatter | solution.py:35
  174.9 2.1 convert_element_type.9
  177.0 1.4 convolution_multiply_fusion.7
  178.4 1.8 fusion.6
  180.2 1.8 fusion.5
  182.1 1.5 fusion.4
  183.6 1.5 fusion.3
  185.1 1.5 fusion.2
  186.6 1.4 fusion.1
  188.0 2.2 fusion.15
  190.4 37.1 %all-gather.5.cloned.1.call-done = bf16[256,8192]{1,0:T(8,128)(2,1)} async-done(((bf16[256,1024]{1,0:T(8,128)(2,1)}), bf16[256,8192]{1,0:T(8,128)(2,1)}) %all-gather.5.cloned.1.call-update) | async-done | bytes 4194320 | tf_op jit(solution)/shard_map/all_gather | solution.py:33
  227.5 28.5 %fusion.75 = f32[256,4096]{1,0:T(8,128)} fusion(bf16[256,8192]{1,0:T(8,128)(2,1)} %all-gather.5.cloned.1.call-done, bf16[8192,4096]{1,0:T(8,128)(2,1)} %bitcast.21), kind=kOutput, calls=%fused_computation.109 | convolution fusion | flops 17179869184 | bytes 75497472 | tf_op jit(solution)/shard_map/dot_general | solution.py:34
  256.1 3.5 all-to-all-start.2
  259.6 73.4 %reduce-scatter.5.cloned.1.call-done = f32[256,1024]{1,0:T(8,128)} async-done(((f32[256,4096]{1,0:T(8,128)}), f32[256,1024]{1,0:T(8,128)}) %reduce-scatter.5.cloned.1.call-update) | async-done | bytes 1048592 | tf_op jit(solution)/shard_map/reduce_scatter | solution.py:35
  334.3 13.2 %all_to_all.51 = bf16[8,32,1024]{2,1,0:T(8,128)(2,1)S(1)} all-to-all(bf16[8,32,1024]{2,1,0:T(8,128)(2,1)S(1)} %bitcast.76), channel_id=1, replica_groups=mesh['dfa'=8,'hid'=4] {'dfa'}, dimensions={0} | all-to-all | bytes 1048576 | tf_op jit(solution)/shard_map/all_to_all | solution.py:36
  347.6 1.5 copy.12
  (52 shorter events, 12.8 us)
Async XLA Ops:
  6.5 8.5 %copy-start = (bf16[64,1,8192]{2,0,1:T(8,128)(2,1)S(1)}, bf16[64,1,8192]{2,0,1:T(8,128)(2,1)}, u32[]{:S(2)}) copy-start(bf16[64,1,8192]{2,0,1:T(8,128)(2,1)} %param.7) | copy-start | bytes 3145732
  8.8 16.0 %all-to-all-start = ((bf16[32,8,1024]{2,0,1:T(8,128)(2,1)}), bf16[32,8,1024]{2,0,1:T(8,128)(2,1)S(1)}, u32[]{:S(2)}, u32[]{:S(2)}) async-start(bf16[32,8,1024]{2,0,1:T(8,128)(2,1)} %bitcast.67), calls=%async_computation | async-start | bytes 1048576 | tf_op jit(solution)/shard_map/all_to_all | solution.py:27
  13.9 9.5 %copy-start.12 = (s32[256,8]{0,1:T(8,128)S(1)}, s32[256,8]{0,1:T(8,128)}, u32[]{:S(2)}) copy-start(s32[256,8]{0,1:T(8,128)} %param.8) | copy-start | bytes 24580
  13.9 55.5 %all-gather.3.cloned.1.call-start = ((), (), s32[]{:S(2)}) async-start(), calls=%async_computation.5 | async-start | bytes 4718592 | tf_op jit(solution)/shard_map/all_gather | solution.py:33
  24.8 2.0 copy-start.11
  25.2 2.1 copy-start.7
  26.8 1.2 copy-start.5
  27.2 1.3 copy-start.3
  27.6 1.4 copy-start.9
  28.4 1.3 copy-start.1
  30.9 144.0 %reduce-scatter.3.cloned.1.call-start = ((), (), s32[]{:S(2)}) async-start(), calls=%async_computation.6 | async-start | bytes 5242880 | tf_op jit(solution)/shard_map/reduce_scatter | solution.py:35
  98.0 129.6 %all-gather.5.cloned.1.call-start = ((), (), s32[]{:S(2)}) async-start(), calls=%async_computation.7 | async-start | bytes 4718592 | tf_op jit(solution)/shard_map/all_gather | solution.py:33
  178.4 3.7 %copy-start.8 = (f32[256,1024]{1,0:T(8,128)S(1)}, f32[256,1024]{1,0:T(8,128)}, u32[]{:S(2)}) copy-start(f32[256,1024]{1,0:T(8,128)} %fusion.24) | copy-start | bytes 3145732
  180.2 3.3 copy-start.6
  182.1 3.0 copy-start.4
  183.6 3.0 copy-start.10
  185.1 2.9 copy-start.2
  190.2 142.8 %reduce-scatter.5.cloned.1.call-start = ((), (), s32[]{:S(2)}) async-start(), calls=%async_computation.8 | async-start | bytes 5242880 | tf_op jit(solution)/shard_map/reduce_scatter | solution.py:35
  256.1 78.2 %all-to-all-start.2 = ((bf16[8,32,1024]{2,1,0:T(8,128)(2,1)}), bf16[8,32,1024]{2,1,0:T(8,128)(2,1)S(1)}, u32[]{:S(2)}, u32[]{:S(2)}) async-start(bf16[8,32,1024]{2,1,0:T(8,128)(2,1)} %bitcast.25), calls=%async_computation.4 | async-start | bytes 1048576 | tf_op jit(solution)/shard_map/all_to_all | solution.py:36
Sparse Core Ops, SparseCore 0:
  31.0 38.3 all-gather.2
  98.1 76.7 reduce-scatter.2
  190.3 37.2 all-gather.4
  256.2 76.7 reduce-scatter.4
where the time goes:
time: 357 us; the launch traced here: 356 us
  waiting for transfers between devices  226 us (63%)
  matrix products  84.6 us (24%)
  between operations  13.5 us (4%)
  blocking collectives  13.2 us (4%)
  starting transfers between devices  9.02 us (3%)
  local copies, waits for them, and re-layouts  5.91 us (2%)
    reduce_scatter x2, waiting for transfers between devices, local(): lax.psum_scatter(part, 'hid', scatter_dimension=1, tiled=True)  150 us
    all_gather x2, waiting for transfers between devices, local(): mixed = lax.all_gather(mixed_own, 'dfa', axis=1, tiled=True)  75.6 us
    dot_general x2, matrix products, local(): part = jnp.dot(mixed, trans_block, preferred_element_type=jnp.float32)  57 us
    dot_general x16, matrix products, edge_mix(): picked = jnp.dot(pick, beta, preferred_element_type=jnp.float32)  17.9 us
    all_to_all x1, blocking collectives, local(): lax.all_to_all(beta, 'dfa', split_axis=0, concat_axis=1, tiled=True)  13.2 us
    dot_general x8, matrix products, edge_mix(): weights = jnp.dot(kind, emission_own, preferred_element_type=jnp.float32)  9.75 us
  transfers between devices with their start and end apart: 6, of which 4 were waited for; matrix products, arithmetic and copies ran while one was open for 3% of the time, Pallas kernels for 0%

commit v1 on v0

--- a/solution.py
+++ b/solution.py
@@ -1,6 +1,10 @@
+import functools
+
 import jax
 import jax.numpy as jnp
 from jax import lax
+from jax.experimental import pallas as pl
+from jax.experimental.pallas import tpu as pltpu
 from jax.sharding import PartitionSpec as P
 
 POS = 2
@@ -16,6 +20,270 @@
         weights = jnp.dot(kind, emission_own, preferred_element_type=jnp.float32)
         total = total + weights * picked
     return total.astype(jnp.bfloat16)
+
+
+PARTS = 2
+SLOTS = 6
+STEP_COLS = 512
+BLOCK_ORDER = (0, 1, 2, 4, 3, 5, 6, 7)
+
+
+def fused_kernel(
+    n_dfa, n_hid,
+    beta_in, w_hbm, emis, succ, tok, out,
+    mixed, weight, pick, rs_send, rs_recv, acc, own, beta, beta_recv, w_slot,
+    a2a_send, a2a_recv, ag_send, ag_recv, sum_send, sum_recv, out_send, out_recv, out_local, w_sem,
+):
+    d, k = lax.axis_index("dfa"), lax.axis_index("hid")
+    core, x, y = lax.rem(d, 2), lax.rem(d // 2, 2), d // 4
+    flips = (1 - 2 * core, 2 - 4 * x, 4 - 8 * y)
+    owned, cells = beta_in.shape[1], beta_in.shape[2]
+    states, degree = succ.shape
+    sub = cells // PARTS
+    out_cols = w_hbm.shape[2]
+    half = states // 2
+    sends = []
+
+    def flip(bits):
+        place = d
+        for bit in range(3):
+            if bits >> bit & 1:
+                place = place + flips[bit]
+        return place
+
+    def remote(source, target, send_sem, recv_sem, where):
+        return pltpu.make_async_remote_copy(
+            src_ref=source, dst_ref=target, send_sem=send_sem, recv_sem=recv_sem,
+            device_id=where, device_id_type=pl.DeviceIdType.MESH,
+        )
+
+    def send(*copy):
+        sends.append(remote(*copy))
+        sends[-1].start()
+
+    order = [(pos, s, i) for pos in range(POS) for s in range(PARTS) for i in range(n_dfa)]
+
+    def w_copy(n):
+        _, s, i = order[n]
+        return pltpu.make_async_copy(
+            w_hbm.at[flip(BLOCK_ORDER[i]), pl.ds(s * sub, sub)], w_slot.at[n % SLOTS], w_sem.at[n % SLOTS]
+        )
+
+    for n in range(SLOTS):
+        w_copy(n).start()
+
+    barrier = pltpu.get_barrier_semaphore()
+    for rel in range(1, n_dfa):
+        pl.semaphore_signal(
+            barrier, inc=1, device_id={"dfa": lax.rem(d + rel, n_dfa)}, device_id_type=pl.DeviceIdType.MESH
+        )
+    for rel in range(1, n_hid):
+        pl.semaphore_signal(
+            barrier, inc=1, device_id={"hid": lax.rem(k + rel, n_hid)}, device_id_type=pl.DeviceIdType.MESH
+        )
+    for j in range(degree):
+        ids = lax.broadcasted_iota(jnp.int32, (states, states), 1)
+        pick[j] = jnp.where(succ[:, j:j + 1] == ids, 1.0, 0.0).astype(jnp.bfloat16)
+    pl.semaphore_wait(barrier, n_dfa - 1 + n_hid - 1)
+
+    def rows_of(device):
+        return pl.ds(pl.multiple_of(device * owned, owned), owned)
+
+    for rel in range(1, n_dfa):
+        other = lax.rem(d + rel, n_dfa)
+        send(beta_in.at[other], beta_recv.at[rows_of(d)], a2a_send.at[rel - 1], a2a_recv.at[rel - 1], {"dfa": other})
+    beta_recv[rows_of(d), :] = beta_in[d]
+    for j in range(degree):
+        sets = lax.broadcasted_iota(jnp.int32, (states, emis.shape[0]), 1)
+        kind = jnp.where(tok[:, j:j + 1] == sets, 1.0, 0.0).astype(jnp.bfloat16)
+        weight[j] = jnp.dot(kind, emis[...], preferred_element_type=jnp.float32).astype(jnp.bfloat16)
+    for rel in range(1, n_dfa):
+        source = lax.rem(d + n_dfa - rel, n_dfa)
+        landed = beta_recv.at[rows_of(source)]
+        remote(landed, landed, a2a_send.at[rel - 1], a2a_recv.at[rel - 1], {"dfa": source}).wait_recv()
+
+    near, along_x, along_y = {"dfa": flip(1)}, {"dfa": flip(2)}, {"dfa": flip(4)}
+    upper, lower = pl.ds(0, half), pl.ds(half, half)
+
+    def gather_send(pos, s, kind, place, where):
+        send(place, place, ag_send.at[pos, s, kind], ag_recv.at[pos, s, kind], where)
+
+    def gather_wait(pos, s, kind, place):
+        remote(place, place, ag_send.at[pos, s, kind], ag_recv.at[pos, s, kind], near).wait_recv()
+
+    def mix(pos, s, values, first):
+        for c in range(0, sub, 256):
+            total = jnp.zeros((states, 256), jnp.float32)
+            for j in range(degree):
+                picked = jnp.dot(pick[j], values[:, first + c:first + c + 256], preferred_element_type=jnp.float32)
+                total = total + weight[j, :, s * sub + c:s * sub + c + 256].astype(jnp.float32) * picked
+            mixed[pos, s, d, :, c:c + 256] = total.astype(jnp.bfloat16)
+        place = mixed.at[pos, s, d]
+        gather_send(pos, s, 1, place, along_x)
+        gather_send(pos, s, 2, place, along_y)
+        gather_send(pos, s, 0, place, near)
+
+    def relay(pos, s):
+        from_x, from_y = mixed.at[pos, s, flip(2)], mixed.at[pos, s, flip(4)]
+        gather_wait(pos, s, 1, from_x)
+        gather_send(pos, s, 3, from_x.at[upper], along_y)
+        gather_send(pos, s, 5, from_x, near)
+        gather_wait(pos, s, 2, from_y)
+        gather_send(pos, s, 4, from_y.at[lower], along_x)
+        gather_send(pos, s, 6, from_y, near)
+
+    def multiply(pos, s):
+        for i, bits in enumerate(BLOCK_ORDER):
+            place = mixed.at[pos, s, flip(bits)]
+            if bits == 1:
+                gather_wait(pos, s, 0, place)
+            if bits == 2:
+                relay(pos, s)
+            if bits == 3:
+                gather_wait(pos, s, 5, place)
+            if bits == 5:
+                gather_wait(pos, s, 6, place)
+            if bits == 6:
+                gather_wait(pos, s, 3, place.at[upper])
+                gather_send(pos, s, 7, place.at[upper], near)
+                gather_wait(pos, s, 4, place.at[lower])
+                gather_send(pos, s, 8, place.at[lower], near)
+            if bits == 7:
+                gather_wait(pos, s, 7, place.at[upper])
+                gather_wait(pos, s, 8, place.at[lower])
+            n = (pos * PARTS + s) * n_dfa + i
+            w_copy(n).wait()
+            slot = n % SLOTS
+
+            def product(cols):
+                return jnp.dot(place[...], w_slot[slot, :, cols], preferred_element_type=jnp.float32)
+
+            if i < n_dfa - 1 or s < PARTS - 1:
+
+                @pl.loop(0, out_cols // STEP_COLS)
+                def _(step):
+                    cols = pl.ds(pl.multiple_of(step * STEP_COLS, STEP_COLS), STEP_COLS)
+                    if s == 0 and i == 0:
+                        acc[:, cols] = product(cols)
+                    else:
+                        acc[:, cols] += product(cols)
+
+            else:
+                for part in range(PARTS):
+                    for rel in (2, 1, 3, 0):
+                        other = lax.rem(k + rel, n_hid)
+                        cols = pl.ds(pl.multiple_of(other * cells + part * sub, sub), sub)
+                        total = acc[:, cols] + product(cols)
+                        if rel == 0:
+                            own[part] = total
+                            continue
+                        rs_send[pos, part, rel - 1] = total.astype(jnp.bfloat16)
+                        send(
+                            rs_send.at[pos, part, rel - 1], rs_recv.at[pos, part, rel - 1],
+                            sum_send.at[pos, part, rel - 1], sum_recv.at[pos, part, rel - 1], {"hid": other},
+                        )
+            if n + SLOTS < len(order):
+                w_copy(n + SLOTS).start()
+
+    def finish_sum(pos, s):
+        total = own[s]
+        for rel in range(1, n_hid):
+            landed = rs_recv.at[pos, s, rel - 1]
+            remote(
+                landed, landed, sum_send.at[pos, s, rel - 1], sum_recv.at[pos, s, rel - 1],
+                {"hid": lax.rem(k + n_hid - rel, n_hid)},
+            ).wait_recv()
+            total = total + landed[...].astype(jnp.float32)
+        beta[pos, s] = total.astype(jnp.bfloat16)
+
+    def local_out(pos, s):
+        return pltpu.make_async_copy(
+            beta.at[pos, s, rows_of(d)], out.at[POS - 1 - pos, s, d], out_local.at[pos, s]
+        )
+
+    def hand_out(pos, s):
+        for rel in range(1, n_dfa):
+            other = lax.rem(d + rel, n_dfa)
+            send(
+                beta.at[pos, s, rows_of(other)], out.at[POS - 1 - pos, s, d],
+                out_send.at[pos, s, rel - 1], out_recv.at[pos, s, rel - 1], {"dfa": other},
+            )
+        local_out(pos, s).start()
+
+    for s in range(PARTS):
+        mix(0, s, beta_recv, s * sub)
+    for s in range(PARTS):
+        multiply(0, s)
+    for pos in range(1, POS):
+        for s in range(PARTS):
+            finish_sum(pos - 1, s)
+            mix(pos, s, beta.at[pos - 1, s], 0)
+            hand_out(pos - 1, s)
+            multiply(pos, s)
+    for s in range(PARTS):
+        finish_sum(POS - 1, s)
+        hand_out(POS - 1, s)
+    for pos in range(POS):
+        for s in range(PARTS):
+            for rel in range(1, n_dfa):
+                source = lax.rem(d + n_dfa - rel, n_dfa)
+                landed = out.at[POS - 1 - pos, s, source]
+                remote(
+                    landed, landed, out_send.at[pos, s, rel - 1], out_recv.at[pos, s, rel - 1], {"dfa": source}
+                ).wait_recv()
+            local_out(pos, s).wait()
+    for copy in sends:
+        copy.wait_send()
+
+
+def fused(n_dfa, n_hid, beta_last, transition, emission, successor, token_set):
+    owned, blocks, _, cells = beta_last.shape
+    states, degree = successor.shape
+    sub = cells // PARTS
+    out_cols = transition.shape[3]
+    first = lax.axis_index("dfa") * cells
+    emission_own = lax.dynamic_slice_in_dim(emission[:, 0, :], first, cells, 1)
+    beta_in = beta_last[:, :, 0, :].transpose(1, 0, 2)
+    w = transition[:, 0]
+    bf16, f32, dma = jnp.bfloat16, jnp.float32, pltpu.SemaphoreType.DMA
+    vmem, anywhere = pl.BlockSpec(memory_space=pltpu.VMEM), pl.BlockSpec(memory_space=pl.ANY)
+    table = pl.pallas_call(
+        functools.partial(fused_kernel, n_dfa, n_hid),
+        out_shape=jax.ShapeDtypeStruct((POS, PARTS, blocks, owned, sub), bf16),
+        in_specs=[vmem, anywhere, vmem, vmem, vmem],
+        out_specs=anywhere,
+        scratch_shapes=[
+            pltpu.VMEM((POS, PARTS, n_dfa, states, sub), bf16),
+            pltpu.VMEM((degree, states, cells), bf16),
+            pltpu.VMEM((degree, states, states), bf16),
+            pltpu.VMEM((POS, PARTS, n_hid - 1, states, sub), bf16),
+            pltpu.VMEM((POS, PARTS, n_hid - 1, states, sub), bf16),
+            pltpu.VMEM((states, out_cols), f32),
+            pltpu.VMEM((PARTS, states, sub), f32),
+            pltpu.VMEM((POS, PARTS, states, sub), bf16),
+            pltpu.VMEM((states, cells), bf16),
+            pltpu.VMEM((SLOTS, sub, out_cols), bf16),
+            dma((n_dfa - 1,)),
+            dma((n_dfa - 1,)),
+            dma((POS, PARTS, 9)),
+            dma((POS, PARTS, 9)),
+            dma((POS, PARTS, n_hid - 1)),
+            dma((POS, PARTS, n_hid - 1)),
+            dma((POS, PARTS, n_dfa - 1)),
+            dma((POS, PARTS, n_dfa - 1)),
+            dma((POS, PARTS)),
+            dma((SLOTS,)),
+        ],
+        compiler_params=pltpu.CompilerParams(
+            collective_id=0, has_side_effects=True, vmem_limit_bytes=60 * 2**20
+        ),
+        cost_estimate=pl.CostEstimate(
+            flops=2 * POS * states * blocks * cells * out_cols,
+            bytes_accessed=2 * POS * blocks * cells * out_cols,
+            transcendentals=0,
+        ),
+    )(beta_in, w, emission_own, successor, token_set)
+    return table.transpose(0, 3, 2, 1, 4).reshape(POS, owned, blocks, 1, cells)
 
 
 def local(beta_last, transition, emission, successor, token_set):
@@ -39,8 +307,16 @@
 
 
 def solution(mesh):
+    n_dfa, n_hid = mesh.shape["dfa"], mesh.shape["hid"]
+
+    def body(beta_last, transition, emission, successor, token_set):
+        owned, blocks, _, cells = beta_last.shape
+        fits = n_dfa == blocks == 8 and n_hid == 4 and cells % (256 * PARTS) == 0 and owned % 16 == 0
+        run = functools.partial(fused, n_dfa, n_hid) if fits else local
+        return run(beta_last, transition, emission, successor, token_set)
+
     return jax.shard_map(
-        local,
+        body,
         mesh=mesh,
         in_specs=(
             P("dfa", None, "hid", None),

time: 357 us -> 190 us (0.53)
  the two profiles are of different devices: /device:TPU:0 before, /device:TPU:19 now
where the time goes in v1:
time: 190 us; the launch traced here: 189 us
  Pallas kernels  178 us (94%)
  local copies, waits for them, and re-layouts  10.8 us (6%)
    pallas_call x1, Pallas kernels, fused(): pl.pallas_call(functools.partial(fused_kernel, n_dfa, n_hid), out_shape=j...  178 us
    unnamed x5, local copies, waits for them, and re-layouts  6.32 us

profile of v1, /device:TPU:19, one launch (start us, length us, event | category | flops | bytes accessed | tf_op | source)
XLA Modules:
  0.0 189.3 jit_solution(13826954633839211907)
XLA Ops:
  0.0 0.0 copy-start
  0.0 1.2 copy-done
  1.2 0.7 dynamic-slice_bitcast_fusion.emis
  1.9 1.5 copy.10.succ
  3.4 1.5 copy.11.tok
  4.9 2.1 %copy.15 = bf16[32,8,1,1024]{3,0,1,2:T(8,128)(2,1)} copy(bf16[32,8,1,1024]{3,1,2,0:T(8,128)(2,1)} %param.5) | data formatting | bytes 1048576 | tf_op args[0]
  7.0 178.5 %shard_map.55 = bf16[2,2,8,32,512]{4,3,2,1,0:T(8,128)(2,1)} custom-call(bf16[8,32,1024]{2,1,0:T(8,128)(2,1)} %bitcast.11, bf16[8,1024,4096]{2,1,0:T(8,128)(2,1)} %bitcast.2.w_hbm, bf16[64,1024]{1,0:T(8,128)(2,1)} %dynamic-slice_bitcast_fusion.emis, s32[256,8]{1,0:T(8,128)} %copy.10.succ, s32[256,8]{1,0:T(8,128)} %copy.11.tok), custom_call_target="tpu_custom_call" | custom-call | flops 34359738368 | bytes 134217728 | tf_op jit(solution)/shard_map/pallas_call | solution.py:250
  185.5 2.3 %copy.12 = bf16[2,32,8,2,512]{4,3,2,1,0:T(2,128)(2,1)S(1)} copy(bf16[2,32,8,2,512]{4,1,2,3,0:T(8,128)(2,1)} %bitcast.10) | data formatting | bytes 2097152 | tf_op jit(solution)/shard_map/transpose | solution.py:286
  187.8 1.5 reshape.4
Async XLA Ops:
  0.0 1.2 copy-start

commit v2 on v1

v2 whole, which is shorter than its diff:
```python
import functools

import jax
import jax.numpy as jnp
from jax import lax
from jax.experimental import pallas as pl
from jax.experimental.pallas import tpu as pltpu
from jax.sharding import PartitionSpec as P

POS = 2


def edge_mix(beta, emission_own, successor, token_set):
    states, nsets = beta.shape[0], emission_own.shape[0]
    total = jnp.zeros(beta.shape, jnp.float32)
    for column in range(successor.shape[1]):
        pick = (successor[:, column][:, None] == jnp.arange(states)[None, :]).astype(jnp.bfloat16)
        kind = (token_set[:, column][:, None] == jnp.arange(nsets)[None, :]).astype(jnp.bfloat16)
        picked = jnp.dot(pick, beta, preferred_element_type=jnp.float32)
        weights = jnp.dot(kind, emission_own, preferred_element_type=jnp.float32)
        total = total + weights * picked
    return total.astype(jnp.bfloat16)


PARTS = 2
SLOTS = 6
BLOCK_ORDER = (0, 1, 2, 4, 3, 5, 6, 7)


def fused_kernel(
    n_dfa, n_hid,
    beta_in, w_hbm, emission, succ, tok, out,
    mixed, weight, pick, rs_send, rs_recv, acc, own, beta, beta_recv, emis, w_slot,
    a2a_send, a2a_recv, ag_send, ag_recv, sum_send, sum_recv, out_send, out_recv, out_local, w_sem, emis_sem,
):
    d, k = lax.axis_index("dfa"), lax.axis_index("hid")
    core, x, y = lax.rem(d, 2), lax.rem(d // 2, 2), d // 4
    flips = (1 - 2 * core, 2 - 4 * x, 4 - 8 * y)
    owned, cells = beta_in.shape[1], beta_in.shape[2]
    degree, states = succ.shape
    sub = cells // PARTS
    groups = w_hbm.shape[2] // sub
    last = PARTS - 1
    half = states // 2
    sends = []

    def flip(bits):
        place = d
        for bit in range(3):
            if bits >> bit & 1:
                place = place + flips[bit]
        return place

    def remote(source, target, send_sem, recv_sem, where):
        return pltpu.make_async_remote_copy(
            src_ref=source, dst_ref=target, send_sem=send_sem, recv_sem=recv_sem,
            device_id=where, device_id_type=pl.DeviceIdType.MESH,
        )

    def send(*copy):
        sends.append(remote(*copy))
        sends[-1].start()

    inner, high = lax.rem((k + 1) // 2, 2), k // 2

    def by_role(at_end, at_inner):
        return at_end + inner * (at_inner - at_end)

    far_end = by_role(3 - k, 3 - 3 * high)
    partner = by_role(1 + high, 3 * high)
    hops = (
        (by_role(far_end, 3 - k), by_role(partner, 3 - k), by_role(1, 3)),
        (by_role(2 - high, partner), by_role(2 - high, partner), by_role(2, 0)),
        (by_role(partner, far_end), by_role(partner, far_end), by_role(0, 1)),
    )
    chunks = [(hops[hop][0], part, hop) for part in range(PARTS) for hop in range(n_hid - 1)]
    chunks += [(k, part, n_hid - 1) for part in range(PARTS)]

    def chunk_cols(chunk):
        block, part, _ = chunk
        return pl.ds(pl.multiple_of(block * cells + part * sub, sub), sub)

    order = [(pos, s, i) for pos in range(POS) for s in range(PARTS) for i in range(n_dfa)]

    def w_column_copy(n):
        _, s, i = order[n]
        return pltpu.make_async_copy(
            w_hbm.at[:, pl.ds(s * sub, sub), chunk_cols(chunks[i])], w_slot.at[n % SLOTS], w_sem.at[n % SLOTS, 0]
        )

    def w_row_copy(n, g):
        _, s, i = order[n]
        cols = pl.ds(pl.multiple_of(g * sub, sub), sub)
        return pltpu.make_async_copy(
            w_hbm.at[flip(BLOCK_ORDER[i]), pl.ds(s * sub, sub), cols],
            w_slot.at[n % SLOTS, g], w_sem.at[n % SLOTS, g],
        )

    def w_start(n):
        if order[n][1] == last:
            w_column_copy(n).start()
        else:
            for g in range(groups):
                w_row_copy(n, g).start()

    emis_copy = pltpu.make_async_copy(
        emission.at[:, pl.ds(pl.multiple_of(d * cells, cells), cells)], emis, emis_sem
    )
    emis_copy.start()
    for n in range(SLOTS):
        w_start(n)

    barrier = pltpu.get_barrier_semaphore()
    for rel in range(1, n_dfa):
        pl.semaphore_signal(
            barrier, inc=1, device_id={"dfa": lax.rem(d + rel, n_dfa)}, device_id_type=pl.DeviceIdType.MESH
        )
    for rel in range(1, n_hid):
        pl.semaphore_signal(
            barrier, inc=1, device_id={"hid": lax.rem(k + rel, n_hid)}, device_id_type=pl.DeviceIdType.MESH
        )
    for j in range(degree):
        ids = lax.broadcasted_iota(jnp.int32, (states, states), 0)
        pick[j] = jnp.where(succ[j:j + 1, :] == ids, 1.0, 0.0).T.astype(jnp.bfloat16)
    pl.semaphore_wait(barrier, n_dfa - 1 + n_hid - 1)

    def rows_of(device):
        return pl.ds(pl.multiple_of(device * owned, owned), owned)

    for rel in range(1, n_dfa):
        other = lax.rem(d + rel, n_dfa)
        send(beta_in.at[other], beta_recv.at[rows_of(d)], a2a_send.at[rel - 1], a2a_recv.at[rel - 1], {"dfa": other})
    beta_recv[rows_of(d), :] = beta_in[d]
    emis_copy.wait()
    for j in range(degree):
        sets = lax.broadcasted_iota(jnp.int32, (emis.shape[0], states), 0)
        kind = jnp.where(tok[j:j + 1, :] == sets, 1.0, 0.0).T.astype(jnp.bfloat16)
        weight[j] = jnp.dot(kind, emis[...], preferred_element_type=jnp.float32).astype(jnp.bfloat16)
    for rel in range(1, n_dfa):
        source = lax.rem(d + n_dfa - rel, n_dfa)
        landed = beta_recv.at[rows_of(source)]
        remote(landed, landed, a2a_send.at[rel - 1], a2a_recv.at[rel - 1], {"dfa": source}).wait_recv()

    near, along_x, along_y = {"dfa": flip(1)}, {"dfa": flip(2)}, {"dfa": flip(4)}
    upper, lower = pl.ds(0, half), pl.ds(half, half)

    def gather_send(pos, s, kind, place, where):
        send(place, place, ag_send.at[pos, s, kind], ag_recv.at[pos, s, kind], where)

    def gather_wait(pos, s, kind, place):
        remote(place, place, ag_send.at[pos, s, kind], ag_recv.at[pos, s, kind], near).wait_recv()

    def mix(pos, s, values, first):
        for c in range(0, sub, 256):
            total = jnp.zeros((states, 256), jnp.float32)
            for j in range(degree):
                picked = jnp.dot(pick[j], values[:, first + c:first + c + 256], preferred_element_type=jnp.float32)
                total = total + weight[j, :, s * sub + c:s * sub + c + 256].astype(jnp.float32) * picked
            mixed[pos, s, d, :, c:c + 256] = total.astype(jnp.bfloat16)
        place = mixed.at[pos, s, d]
        gather_send(pos, s, 1, place, along_x)
        gather_send(pos, s, 2, place, along_y)
        gather_send(pos, s, 0, place, near)

    def relay(pos, s):
        from_x, from_y = mixed.at[pos, s, flip(2)], mixed.at[pos, s, flip(4)]
        gather_wait(pos, s, 1, from_x)
        gather_send(pos, s, 3, from_x.at[upper], along_y)
        gather_send(pos, s, 5, from_x, near)
        gather_wait(pos, s, 2, from_y)
        gather_send(pos, s, 4, from_y.at[lower], along_x)
        gather_send(pos, s, 6, from_y, near)

    def arrive(pos, s, bits):
        place = mixed.at[pos, s, flip(bits)]
        if bits == 1:
            gather_wait(pos, s, 0, place)
        if bits == 3:
            gather_wait(pos, s, 5, place)
        if bits == 5:
            gather_wait(pos, s, 6, place)
        if bits == 6:
            gather_wait(pos, s, 3, place.at[upper])
            gather_send(pos, s, 7, place.at[upper], near)
            gather_wait(pos, s, 4, place.at[lower])
            gather_send(pos, s, 8, place.at[lower], near)
        if bits == 7:
            gather_wait(pos, s, 7, place.at[upper])
            gather_wait(pos, s, 8, place.at[lower])

    def multiply_rows(pos, s, relay_next):
        for i, bits in enumerate(BLOCK_ORDER):
            if bits == 2:
                relay(pos, s)
            if bits == 3 and relay_next:
                relay(pos, s + 1)
            arrive(pos, s, bits)
            place = mixed.at[pos, s, flip(bits)]
            n = (pos * PARTS + s) * n_dfa + i
            slot = n % SLOTS

            @pl.loop(0, groups)
            def _(g):
                w_row_copy(n, g).wait()
                cols = pl.ds(pl.multiple_of(g * sub, sub), sub)
                product = jnp.dot(place[...], w_slot[slot, g], preferred_element_type=jnp.float32)
                if s == 0 and i == 0:
                    acc[:, cols] = product
                else:
                    acc[:, cols] += product

            if n + SLOTS < len(order):
                w_start(n + SLOTS)

    def sum_copy(pos, part, hop):
        _, device, slot = hops[hop]
        return (
            rs_send.at[pos, part, hop], rs_recv.at[pos, part, slot],
            sum_send.at[pos, part, hop], sum_recv.at[pos, part, slot], {"hid": device},
        )

    def sum_wait(pos, part, slot):
        landed = rs_recv.at[pos, part, slot]
        remote(landed, landed, sum_send.at[pos, part, 0], sum_recv.at[pos, part, slot], {"hid": partner}).wait_recv()
        return landed

    def multiply_columns(pos, relay_first):
        if relay_first:
            relay(pos, last)
        for bits in BLOCK_ORDER:
            arrive(pos, last, bits)
        for i, chunk in enumerate(chunks):
            _, part, hop = chunk
            n = (pos * PARTS + last) * n_dfa + i
            slot = n % SLOTS
            cols = chunk_cols(chunk)
            w_column_copy(n).wait()

            @pl.loop(0, n_dfa)
            def _(a):
                acc[:, cols] += jnp.dot(mixed[pos, last, a], w_slot[slot, a], preferred_element_type=jnp.float32)

            if n + SLOTS < len(order):
                w_start(n + SLOTS)
            if hop == n_hid - 1:
                own[part] = acc[:, cols]
                continue
            if hop == n_hid - 2:

                @pl.when(inner == 1)
                def _():
                    acc[:, cols] += sum_wait(pos, part, 1)[...].astype(jnp.float32)

            rs_send[pos, part, hop] = acc[:, cols].astype(jnp.bfloat16)
            send(*sum_copy(pos, part, hop))

    def finish_sum(pos, s):
        own[s] += sum_wait(pos, s, 0)[...].astype(jnp.float32)

        @pl.when(inner == 0)
        def _():
            own[s] += sum_wait(pos, s, 1)[...].astype(jnp.float32)

        @pl.when(inner == 1)
        def _():
            for slot in (3, 2):
                own[s] += sum_wait(pos, s, slot)[...].astype(jnp.float32)

        beta[pos, s] = own[s].astype(jnp.bfloat16)

    def out_place(pos, s, block):
        return out.at[POS - 1 - pos, block, :, pl.ds(s * sub, sub)]

    def local_out(pos, s):
        return pltpu.make_async_copy(
            beta.at[pos, s, rows_of(d)], out_place(pos, s, d), out_local.at[pos, s]
        )

    def hand_out(pos, s):
        for rel in range(1, n_dfa):
            other = lax.rem(d + rel, n_dfa)
            send(
                beta.at[pos, s, rows_of(other)], out_place(pos, s, d),
                out_send.at[pos, s, rel - 1], out_recv.at[pos, s, rel - 1], {"dfa": other},
            )
        local_out(pos, s).start()

    for s in range(PARTS):
        mix(0, s, beta_recv, s * sub)
    for s in range(last):
        multiply_rows(0, s, True)
    multiply_columns(0, False)
    for pos in range(1, POS):
        for s in range(PARTS):
            finish_sum(pos - 1, s)
            mix(pos, s, beta.at[pos - 1, s], 0)
            hand_out(pos - 1, s)
            if s < last:
                multiply_rows(pos, s, False)
            else:
                multiply_columns(pos, True)
    for s in range(PARTS):
        finish_sum(POS - 1, s)
        hand_out(POS - 1, s)
    for pos in range(POS):
        for s in range(PARTS):
            for rel in range(1, n_dfa):
                source = lax.rem(d + n_dfa - rel, n_dfa)
                landed = out_place(pos, s, source)
                remote(
                    landed, landed, out_send.at[pos, s, rel - 1], out_recv.at[pos, s, rel - 1], {"dfa": source}
                ).wait_recv()
            local_out(pos, s).wait()
    for copy in sends:
        copy.wait_send()


def fused(n_dfa, n_hid, beta_last, transition, emission, successor, token_set):
    owned, blocks, _, cells = beta_last.shape
    states, degree = successor.shape
    sub = cells // PARTS
    out_cols = transition.shape[3]
    beta_in = beta_last[:, :, 0, :].transpose(1, 0, 2)
    w = transition[:, 0]
    bf16, f32, dma = jnp.bfloat16, jnp.float32, pltpu.SemaphoreType.DMA
    vmem, anywhere = pl.BlockSpec(memory_space=pltpu.VMEM), pl.BlockSpec(memory_space=pl.ANY)
    table = pl.pallas_call(
        functools.partial(fused_kernel, n_dfa, n_hid),
        out_shape=jax.ShapeDtypeStruct((POS, blocks, owned, cells), bf16),
        in_specs=[vmem, anywhere, anywhere, vmem, vmem],
        out_specs=anywhere,
        scratch_shapes=[
            pltpu.VMEM((POS, PARTS, n_dfa, states, sub), bf16),
            pltpu.VMEM((degree, states, cells), bf16),
            pltpu.VMEM((degree, states, states), bf16),
            pltpu.VMEM((POS, PARTS, n_hid - 1, states, sub), bf16),
            pltpu.VMEM((POS, PARTS, n_hid, states, sub), bf16),
            pltpu.VMEM((states, out_cols), f32),
            pltpu.VMEM((PARTS, states, sub), f32),
            pltpu.VMEM((POS, PARTS, states, sub), bf16),
            pltpu.VMEM((states, cells), bf16),
            pltpu.VMEM((emission.shape[0], cells), bf16),
            pltpu.VMEM((SLOTS, n_dfa, sub, sub), bf16),
            dma((n_dfa - 1,)),
            dma((n_dfa - 1,)),
            dma((POS, PARTS, 9)),
            dma((POS, PARTS, 9)),
            dma((POS, PARTS, n_hid - 1)),
            dma((POS, PARTS, n_hid)),
            dma((POS, PARTS, n_dfa - 1)),
            dma((POS, PARTS, n_dfa - 1)),
            dma((POS, PARTS)),
            dma((SLOTS, n_dfa)),
            dma,
        ],
        compiler_params=pltpu.CompilerParams(
            collective_id=0, has_side_effects=True, vmem_limit_bytes=60 * 2**20
        ),
        cost_estimate=pl.CostEstimate(
            flops=2 * POS * states * blocks * cells * out_cols,
            bytes_accessed=2 * POS * blocks * cells * out_cols,
            transcendentals=0,
        ),
    )(beta_in, w, emission[:, 0, :], successor.T, token_set.T)
    return table.transpose(0, 2, 1, 3).reshape(POS, owned, blocks, 1, cells)


def local(beta_last, transition, emission, successor, token_set):
    owned, blocks, _, cells = beta_last.shape
    width = blocks * cells
    trans_block = transition.reshape(width, transition.shape[3])
    first = lax.axis_index("dfa") * cells
    emission_own = lax.dynamic_slice_in_dim(emission[:, 0, :], first, cells, 1)
    beta = lax.all_to_all(
        beta_last.reshape(owned, width), "dfa", split_axis=1, concat_axis=0, tiled=True
    )
    results = []
    for position in range(POS):
        mixed_own = edge_mix(beta, emission_own, successor, token_set)
        mixed = lax.all_gather(mixed_own, "dfa", axis=1, tiled=True)
        part = jnp.dot(mixed, trans_block, preferred_element_type=jnp.float32)
        beta = lax.psum_scatter(part, "hid", scatter_dimension=1, tiled=True).astype(jnp.bfloat16)
        own_rows = lax.all_to_all(beta, "dfa", split_axis=0, concat_axis=1, tiled=True)
        results = [own_rows.reshape(owned, blocks, 1, cells)] + results
    return jnp.stack(results)


def solution(mesh):
    n_dfa, n_hid = mesh.shape["dfa"], mesh.shape["hid"]

    def body(beta_last, transition, emission, successor, token_set):
        owned, blocks, _, cells = beta_last.shape
        fits = n_dfa == blocks == 8 and n_hid == 4 and PARTS == 2 and cells % (256 * PARTS) == 0 and owned % 16 == 0
        fits = fits and transition.shape[3] == n_hid * cells
        run = functools.partial(fused, n_dfa, n_hid) if fits else local
        return run(beta_last, transition, emission, successor, token_set)

    return jax.shard_map(
        body,
        mesh=mesh,
        in_specs=(
            P("dfa", None, "hid", None),
            P(None, "hid", None, "dfa"),
            P(None, "hid", None),
            P(),
            P(),
        ),
        out_specs=P(None, "dfa", None, "hid", None),
        check_vma=False,
    )
```

time: 190 us -> 158 us (0.83)
  the two profiles are of different devices: /device:TPU:19 before, /device:TPU:0 now
where the time goes in v2:
time: 158 us
  Pallas kernels  153 us (97%)
  local copies, waits for them, and re-layouts  4.9 us (3%)
    pallas_call x1, Pallas kernels, fused(): pl.pallas_call(functools.partial(fused_kernel, n_dfa, n_hid), out_shape=j...  153 us

profile of v2, /device:TPU:0, one launch (start us, length us, event | category | flops | bytes accessed | tf_op | source)
XLA Modules:
  0.0 157.6 jit_solution(16481370867916677211)
XLA Ops:
  0.0 2.1 %copy.9 = bf16[32,8,1,1024]{3,0,1,2:T(8,128)(2,1)} copy(bf16[32,8,1,1024]{3,1,2,0:T(8,128)(2,1)} %param.5) | data formatting | bytes 1048576 | tf_op args[0]
  2.1 152.7 %shard_map.55 = bf16[2,8,32,1024]{3,2,1,0:T(8,128)(2,1)} custom-call(bf16[8,32,1024]{2,1,0:T(8,128)(2,1)} %bitcast.13, bf16[8,1024,4096]{2,1,0:T(8,128)(2,1)} %bitcast.2.w_hbm, bf16[64,8192]{1,0:T(8,128)(2,1)} %bitcast.14, s32[8,256]{1,0:T(8,128)} %bitcast.15, s32[8,256]{1,0:T(8,128)} %bitcast.16), custom_call_target="tpu_custom_call" | custom-call | flops 34359738368 | bytes 134217728 | tf_op jit(solution)/shard_map/pallas_call | solution.py:327
  154.8 2.8 %copy.7 = bf16[2,32,8,1,1024]{4,2,3,1,0:T(8,128)(2,1)} copy(bf16[2,32,8,1,1024]{4,1,2,0,3:T(8,128)(2,1)} %bitcast.12) | data formatting | bytes 2097152 | tf_op jit(solution)/shard_map/reshape | solution.py:365

commit v3 on v2

--- a/solution.py
+++ b/solution.py
@@ -127,19 +127,26 @@
     def rows_of(device):
         return pl.ds(pl.multiple_of(device * owned, owned), owned)
 
-    for rel in range(1, n_dfa):
-        other = lax.rem(d + rel, n_dfa)
-        send(beta_in.at[other], beta_recv.at[rows_of(d)], a2a_send.at[rel - 1], a2a_recv.at[rel - 1], {"dfa": other})
+    for s in range(PARTS):
+        cols = pl.ds(s * sub, sub)
+        for rel in range(1, n_dfa):
+            other = lax.rem(d + rel, n_dfa)
+            send(
+                beta_in.at[other, :, cols], beta_recv.at[rows_of(d), cols],
+                a2a_send.at[s, rel - 1], a2a_recv.at[s, rel - 1], {"dfa": other},
+            )
     beta_recv[rows_of(d), :] = beta_in[d]
     emis_copy.wait()
     for j in range(degree):
         sets = lax.broadcasted_iota(jnp.int32, (emis.shape[0], states), 0)
         kind = jnp.where(tok[j:j + 1, :] == sets, 1.0, 0.0).T.astype(jnp.bfloat16)
         weight[j] = jnp.dot(kind, emis[...], preferred_element_type=jnp.float32).astype(jnp.bfloat16)
-    for rel in range(1, n_dfa):
-        source = lax.rem(d + n_dfa - rel, n_dfa)
-        landed = beta_recv.at[rows_of(source)]
-        remote(landed, landed, a2a_send.at[rel - 1], a2a_recv.at[rel - 1], {"dfa": source}).wait_recv()
+
+    def beta_wait(s):
+        for rel in range(1, n_dfa):
+            source = lax.rem(d + n_dfa - rel, n_dfa)
+            landed = beta_recv.at[rows_of(source), pl.ds(s * sub, sub)]
+            remote(landed, landed, a2a_send.at[s, rel - 1], a2a_recv.at[s, rel - 1], {"dfa": source}).wait_recv()
 
     near, along_x, along_y = {"dfa": flip(1)}, {"dfa": flip(2)}, {"dfa": flip(4)}
     upper, lower = pl.ds(0, half), pl.ds(half, half)
@@ -158,17 +165,21 @@
                 total = total + weight[j, :, s * sub + c:s * sub + c + 256].astype(jnp.float32) * picked
             mixed[pos, s, d, :, c:c + 256] = total.astype(jnp.bfloat16)
         place = mixed.at[pos, s, d]
-        gather_send(pos, s, 1, place, along_x)
-        gather_send(pos, s, 2, place, along_y)
+        gather_send(pos, s, 1, place.at[upper], along_x)
+        gather_send(pos, s, 2, place.at[lower], along_y)
+        gather_send(pos, s, 9, place.at[lower], along_x)
+        gather_send(pos, s, 10, place.at[upper], along_y)
         gather_send(pos, s, 0, place, near)
 
     def relay(pos, s):
         from_x, from_y = mixed.at[pos, s, flip(2)], mixed.at[pos, s, flip(4)]
-        gather_wait(pos, s, 1, from_x)
+        gather_wait(pos, s, 1, from_x.at[upper])
         gather_send(pos, s, 3, from_x.at[upper], along_y)
+        gather_wait(pos, s, 2, from_y.at[lower])
+        gather_send(pos, s, 4, from_y.at[lower], along_x)
+        gather_wait(pos, s, 9, from_x.at[lower])
         gather_send(pos, s, 5, from_x, near)
-        gather_wait(pos, s, 2, from_y)
-        gather_send(pos, s, 4, from_y.at[lower], along_x)
+        gather_wait(pos, s, 10, from_y.at[upper])
         gather_send(pos, s, 6, from_y, near)
 
     def arrive(pos, s, bits):
@@ -286,6 +297,7 @@
         local_out(pos, s).start()
 
     for s in range(PARTS):
+        beta_wait(s)
         mix(0, s, beta_recv, s * sub)
     for s in range(last):
         multiply_rows(0, s, True)
@@ -294,11 +306,12 @@
         for s in range(PARTS):
             finish_sum(pos - 1, s)
             mix(pos, s, beta.at[pos - 1, s], 0)
-            hand_out(pos - 1, s)
             if s < last:
                 multiply_rows(pos, s, False)
             else:
                 multiply_columns(pos, True)
+        for s in range(PARTS):
+            hand_out(pos - 1, s)
     for s in range(PARTS):
         finish_sum(POS - 1, s)
         hand_out(POS - 1, s)
@@ -341,10 +354,10 @@
             pltpu.VMEM((states, cells), bf16),
             pltpu.VMEM((emission.shape[0], cells), bf16),
             pltpu.VMEM((SLOTS, n_dfa, sub, sub), bf16),
-            dma((n_dfa - 1,)),
-            dma((n_dfa - 1,)),
-            dma((POS, PARTS, 9)),
-            dma((POS, PARTS, 9)),
+            dma((PARTS, n_dfa - 1)),
+            dma((PARTS, n_dfa - 1)),
+            dma((POS, PARTS, 11)),
+            dma((POS, PARTS, 11)),
             dma((POS, PARTS, n_hid - 1)),
             dma((POS, PARTS, n_hid)),
             dma((POS, PARTS, n_dfa - 1)),

time: 158 us -> 152 us (0.962)
  Pallas kernels: 153 us -> 147 us
    pallas_call x1, Pallas kernels: 153 us -> 147 us  [fused(): pl.pallas_call(functools.partial(fused_kernel, n_dfa, n_hid), out_shape=j...]
where the time goes in v3:
time: 152 us
  Pallas kernels  147 us (97%)
  local copies, waits for them, and re-layouts  4.9 us (3%)
    pallas_call x1, Pallas kernels, fused(): pl.pallas_call(functools.partial(fused_kernel, n_dfa, n_hid), out_shape=j...  147 us

profile of v3, /device:TPU:0, one launch (start us, length us, event | category | flops | bytes accessed | tf_op | source)
XLA Modules:
  0.0 151.6 jit_solution(306946371255407178)
XLA Ops:
  0.0 2.1 %copy.9 = bf16[32,8,1,1024]{3,0,1,2:T(8,128)(2,1)} copy(bf16[32,8,1,1024]{3,1,2,0:T(8,128)(2,1)} %param.5) | data formatting | bytes 1048576 | tf_op args[0]
  2.1 146.7 %shard_map.55 = bf16[2,8,32,1024]{3,2,1,0:T(8,128)(2,1)} custom-call(bf16[8,32,1024]{2,1,0:T(8,128)(2,1)} %bitcast.13, bf16[8,1024,4096]{2,1,0:T(8,128)(2,1)} %bitcast.2.w_hbm, bf16[64,8192]{1,0:T(8,128)(2,1)} %bitcast.14, s32[8,256]{1,0:T(8,128)} %bitcast.15, s32[8,256]{1,0:T(8,128)} %bitcast.16), custom_call_target="tpu_custom_call" | custom-call | flops 34359738368 | bytes 134217728 | tf_op jit(solution)/shard_map/pallas_call | solution.py:340
  148.9 2.8 %copy.7 = bf16[2,32,8,1,1024]{4,2,3,1,0:T(8,128)(2,1)} copy(bf16[2,32,8,1,1024]{4,1,2,0,3:T(8,128)(2,1)} %bitcast.12) | data formatting | bytes 2097152 | tf_op jit(solution)/shard_map/reshape | solution.py:378
